TPU v7x, 256 devices: a whole 4x4x8 slice. The times are simulated.
256 devices in a mesh: section: 16 (over z_lo, y), dp: 16 (over x, z_hi, core).
Axes of the slice: x: 4, y: 4, z: 8 (z_hi: 2, z_lo: 4; z = z_hi * 4 + z_lo), core: 2. Of those that a mesh axis runs over, the one named last changes fastest.
Arguments:
- layer_inputs: bfloat16 [16, 2, 64, 4096], P('section'), may hold values from -6 to 6
- top_grad: bfloat16 [2, 64, 4096], replicated, may hold values from -3 to 3
- w_query: bfloat16 [16, 4096, 4096], P('section', None, 'dp'), may hold values from -1 to 1
- w_keyval: bfloat16 [16, 4096, 1024], P('section', None, 'dp'), may hold values from -1 to 1
- w_out: bfloat16 [16, 4096, 4096], P('section', 'dp'), may hold values from -0.02734375 to 0.02734375
- norm_gain: bfloat16 [16, 4096], P('section'), may hold values from 0.25 to 1.75
- new_block: int32 [16], P('section'), may hold values 0 or 1
Outputs:
- grad_stream: bfloat16 [16, 2, 64, 4096], P('section', None, None, 'dp')
- grad_out_proj: float32 [16, 4096, 4096], P('section', 'dp')
All inputs are finite; a program needn't handle non-finite values. No bound on the sum of `new_block` on one device may be relied on, other than what follows from the above.
Results may differ from a plain program's by a relative error of at most 0.035.
Values may be sent and summed in bfloat16 or wider, within the bound.
A program may use at most 64 MiB of HBM per device.

v0:
```python
import jax
import jax.numpy as jnp
from jax import lax
from jax.sharding import PartitionSpec as P

KVH = 4
HEAD_DIM = 128
EPS = 1e-05


def swapped(value, axis, distance):
    mask = 2**distance
    pairs = [(source, source ^ mask) for source in range(lax.axis_size(axis))]
    return lax.ppermute(value, axis, pairs)


def shifted(value, axis, by):
    count = lax.axis_size(axis)
    pairs = [(i, i + by) for i in range(count) if 0 <= i + by < count]
    return lax.ppermute(value, axis, pairs)


def body(layer_inputs, top_grad, w_query, w_keyval, w_out, norm_gain, new_block):
    dp_count = lax.axis_size("dp")
    section_count = lax.axis_size("section")
    dp_pos = lax.axis_index("dp")
    section_pos = lax.axis_index("section")
    micro_count = layer_inputs.shape[1]
    tokens = layer_inputs.shape[2]
    width = layer_inputs.shape[3]
    slice_width = width // dp_count
    query_local = w_query[0]
    out_local = w_out[0]
    gain = norm_gain[0].astype(jnp.float32)
    is_new = new_block[0] == 1
    scale_factor = HEAD_DIM ** (-0.5)
    local_heads = query_local.shape[1] // HEAD_DIM
    head_cols = w_keyval[0]
    for bit_pos in range((dp_count // KVH).bit_length() - 1):
        partner = swapped(head_cols, "dp", bit_pos)
        lower = dp_pos // 2**bit_pos % 2 == 0
        head_cols = jnp.where(
            lower,
            jnp.concatenate([head_cols, partner], 1),
            jnp.concatenate([partner, head_cols], 1),
        )
    causal = jnp.arange(tokens)[:, None] >= jnp.arange(tokens)[None, :]
    col_start = dp_pos * slice_width
    top_section = section_pos == section_count - 1

    def layer_terms(inputs, upstream):
        inputs_f = inputs.astype(jnp.float32)
        inverse_rms = lax.rsqrt(jnp.mean(inputs_f * inputs_f, axis=-1, keepdims=True) + EPS)
        normed = (inputs_f * inverse_rms * gain).astype(jnp.bfloat16)
        queries = jnp.dot(normed, query_local, preferred_element_type=jnp.float32).astype(
            jnp.bfloat16
        )
        queries = queries.reshape(tokens, local_heads, HEAD_DIM)
        keyval = jnp.dot(normed, head_cols, preferred_element_type=jnp.float32).astype(jnp.bfloat16)
        key_rows = keyval[:, :HEAD_DIM]
        value_rows = keyval[:, HEAD_DIM:]
        scores = (
            jnp.einsum("thd,sd->hts", queries, key_rows, preferred_element_type=jnp.float32)
            * scale_factor
        )
        scores = jnp.where(causal[None], scores, -1e30)
        probs = jax.nn.softmax(scores, axis=-1)
        probs_low = probs.astype(jnp.bfloat16)
        attended = jnp.einsum(
            "hts,sd->thd", probs_low, value_rows, preferred_element_type=jnp.float32
        ).astype(jnp.bfloat16)
        attended_flat = attended.reshape(tokens, local_heads * HEAD_DIM)
        out_grad = jnp.einsum(
            "tc,kc->tk", upstream, out_local, preferred_element_type=jnp.float32
        ).astype(jnp.bfloat16)
        out_grad = out_grad.reshape(tokens, local_heads, HEAD_DIM)
        weight_grad = jnp.einsum(
            "tk,tc->kc", attended_flat, upstream, preferred_element_type=jnp.float32
        )
        prob_grad = jnp.einsum(
            "thd,sd->hts", out_grad, value_rows, preferred_element_type=jnp.float32
        )
        row_delta = jnp.sum(probs * prob_grad, axis=-1, keepdims=True)
        score_low = (probs * (prob_grad - row_delta)).astype(jnp.bfloat16)
        query_grad = (
            jnp.einsum("hts,sd->thd", score_low, key_rows, preferred_element_type=jnp.float32)
            * scale_factor
        )
        query_grad = query_grad.astype(jnp.bfloat16).reshape(tokens, local_heads * HEAD_DIM)
        key_grad = (
            jnp.einsum("hts,thd->sd", score_low, queries, preferred_element_type=jnp.float32)
            * scale_factor
        )
        value_grad = jnp.einsum(
            "hts,thd->sd", probs_low, out_grad, preferred_element_type=jnp.float32
        )
        keyval_grad = jnp.concatenate([key_grad, value_grad], axis=-1).astype(jnp.bfloat16)
        partial_value = jnp.einsum(
            "tk,ck->tc", query_grad, query_local, preferred_element_type=jnp.float32
        )
        partial_value = partial_value + jnp.einsum(
            "tk,ck->tc", keyval_grad, head_cols, preferred_element_type=jnp.float32
        )
        return (partial_value, weight_grad, inputs_f, inverse_rms)

    def backward_step(step_pos, received):
        micro_pos = step_pos - (section_count - 1 - section_pos)
        active = (micro_pos >= 0) & (micro_pos < micro_count)
        micro_clip = jnp.clip(micro_pos, 0, micro_count - 1)
        inputs = lax.dynamic_index_in_dim(layer_inputs[0], micro_clip, 0, keepdims=False)
        from_top = lax.dynamic_index_in_dim(top_grad, micro_clip, 0, keepdims=False)
        upstream = jnp.where(top_section, from_top, received)
        partial_value, weight_grad, inputs_f, inverse_rms = layer_terms(inputs, upstream)
        summed = lax.psum_scatter(
            partial_value.astype(jnp.bfloat16), "dp", scatter_dimension=1, tiled=True
        )
        return (summed, upstream, weight_grad, inputs_f, inverse_rms, micro_clip, active)

    def record(stream_acc, grad_acc, result_part, weight_grad, micro_clip, active):
        old_row = lax.dynamic_index_in_dim(stream_acc, micro_clip, 0, keepdims=False)
        new_row = jnp.where(active, result_part, old_row)
        stream_acc = lax.dynamic_update_index_in_dim(stream_acc, new_row, micro_clip, 0)
        grad_acc = grad_acc + jnp.where(active & is_new, weight_grad, 0.0)
        return (stream_acc, grad_acc)

    stream_init = jnp.zeros((micro_count, tokens, slice_width), jnp.bfloat16)
    grad_init = jnp.zeros((out_local.shape[0], width), jnp.float32)
    tick_count = micro_count + section_count - 1

    def tick_whole(step_pos, carry):
        incoming, stream_acc, grad_acc = carry
        norm_part, upstream, weight_grad, inputs_f, inverse_rms, micro_clip, active = backward_step(
            step_pos, incoming
        )
        norm_grad = lax.all_gather(norm_part, "dp", axis=1, tiled=True).astype(jnp.float32)
        scaled = norm_grad * gain
        row_stat = jnp.sum(scaled * inputs_f, axis=-1, keepdims=True) / width
        result = (
            upstream.astype(jnp.float32)
            + inverse_rms * scaled
            - inputs_f * inverse_rms**3 * row_stat
        ).astype(jnp.bfloat16)
        outgoing = shifted(result, "section", -1)
        result_part = lax.dynamic_slice_in_dim(result, col_start, slice_width, 1)
        stream_acc, grad_acc = record(
            stream_acc, grad_acc, result_part, weight_grad, micro_clip, active
        )
        return (outgoing, stream_acc, grad_acc)

    start = jnp.zeros((tokens, width), jnp.bfloat16)
    carry = lax.fori_loop(0, tick_count, tick_whole, (start, stream_init, grad_init))
    return (carry[1][None], carry[2][None])


def solution(mesh):
    in_specs = (
        P("section", None, None, None),
        P(),
        P("section", None, "dp"),
        P("section", None, "dp"),
        P("section", "dp", None),
        P("section", None),
        P("section"),
    )
    out_specs = (P("section", None, None, "dp"), P("section", "dp", None))
    return jax.shard_map(body, mesh=mesh, in_specs=in_specs, out_specs=out_specs, check_vma=False)
```

profile of v0, /device:TPU:88, one launch (start us, length us, event | category | flops | bytes accessed | tf_op | source)
XLA Modules:
  0.0 2371.7 jit_solution(1513456460127013355)
XLA Ops:
  17.0 45.7 %collective-permute-done.2 = bf16[4096,128]{0,1:T(8,128)(2,1)S(1)} collective-permute-done((bf16[4096,128]{0,1:T(8,128)(2,1)S(1)}, bf16[4096,128]{0,1:T(8,128)(2,1)S(1)}, u32[]{:S(2)}, u32[]{:S(2)}) %collective-permute-start.2) | collective-permute-done | bytes 1048608 | tf_op jit(solution)/shard_map/ppermute | solution.py:14
  67.9 2296.6 %while.20 = (s32[]{:T(128)}, bf16[64,4096]{1,0:T(8,128)(2,1)S(1)}, bf16[2,64,256]{2,1,0:T(8,128)(2,1)S(1)}, f32[256,4096]{1,0:T(8,128)}, pred[]{:T(512)}, /*inde...) while((s32[]{:T(128)}, bf16[64,4096]{1,0:T(8,128)(2,1)S(1)}, ...), condition=%wide.region_7.8_spmd.clone, body=%wide.region_0.7_spmd.clone.sunk | while | flops 828969088 | bytes 55234480 | solution.py:151
  78.9 76.2 %reduce-scatter.2.cloned.1.call-done = bf16[64,256]{1,0:T(8,128)(2,1)} async-done(((bf16[64,4096]{1,0:T(8,128)(2,1)}), bf16[64,256]{1,0:T(8,128)(2,1)}) %reduce-scatter.2.cloned.1.call-update) | async-done | bytes 32784 | tf_op jit(solution)/shard_map/while/body/eval_jaxpr/reduce_scatter | solution.py:114
  218.9 71.0 %reduce-scatter.2.cloned.1.call-done = bf16[64,256]{1,0:T(8,128)(2,1)} async-done(((bf16[64,4096]{1,0:T(8,128)(2,1)}), bf16[64,256]{1,0:T(8,128)(2,1)}) %reduce-scatter.2.cloned.1.call-update) | async-done | bytes 32784 | tf_op jit(solution)/shard_map/while/body/eval_jaxpr/reduce_scatter | solution.py:114
  353.8 71.0 %reduce-scatter.2.cloned.1.call-done = bf16[64,256]{1,0:T(8,128)(2,1)} async-done(((bf16[64,4096]{1,0:T(8,128)(2,1)}), bf16[64,256]{1,0:T(8,128)(2,1)}) %reduce-scatter.2.cloned.1.call-update) | async-done | bytes 32784 | tf_op jit(solution)/shard_map/while/body/eval_jaxpr/reduce_scatter | solution.py:114
  424.8 32.0 %all_gather.11 = bf16[64,4096]{1,0:T(8,128)(2,1)S(1)} all-gather(bf16[64,256]{1,0:T(8,128)(2,1)} %reduce-scatter.2.cloned.1.call-done), channel_id=1, replica_groups=mesh['section'=16,'dp'=16] {'dp'}, dimensions={1}, use_global_device_ids=true | all-gather | bytes 557056 | tf_op jit(solution)/shard_map/while/body/eval_jaxpr/all_gather | solution.py:135
  488.7 70.7 %reduce-scatter.2.cloned.1.call-done = bf16[64,256]{1,0:T(8,128)(2,1)} async-done(((bf16[64,4096]{1,0:T(8,128)(2,1)}), bf16[64,256]{1,0:T(8,128)(2,1)}) %reduce-scatter.2.cloned.1.call-update) | async-done | bytes 32784 | tf_op jit(solution)/shard_map/while/body/eval_jaxpr/reduce_scatter | solution.py:114
  559.3 32.0 %all_gather.11 = bf16[64,4096]{1,0:T(8,128)(2,1)S(1)} all-gather(bf16[64,256]{1,0:T(8,128)(2,1)} %reduce-scatter.2.cloned.1.call-done), channel_id=1, replica_groups=mesh['section'=16,'dp'=16] {'dp'}, dimensions={1}, use_global_device_ids=true | all-gather | bytes 557056 | tf_op jit(solution)/shard_map/while/body/eval_jaxpr/all_gather | solution.py:135
  623.2 71.0 %reduce-scatter.2.cloned.1.call-done = bf16[64,256]{1,0:T(8,128)(2,1)} async-done(((bf16[64,4096]{1,0:T(8,128)(2,1)}), bf16[64,256]{1,0:T(8,128)(2,1)}) %reduce-scatter.2.cloned.1.call-update) | async-done | bytes 32784 | tf_op jit(solution)/shard_map/while/body/eval_jaxpr/reduce_scatter | solution.py:114
  694.2 32.0 %all_gather.11 = bf16[64,4096]{1,0:T(8,128)(2,1)S(1)} all-gather(bf16[64,256]{1,0:T(8,128)(2,1)} %reduce-scatter.2.cloned.1.call-done), channel_id=1, replica_groups=mesh['section'=16,'dp'=16] {'dp'}, dimensions={1}, use_global_device_ids=true | all-gather | bytes 557056 | tf_op jit(solution)/shard_map/while/body/eval_jaxpr/all_gather | solution.py:135
  758.1 70.6 %reduce-scatter.2.cloned.1.call-done = bf16[64,256]{1,0:T(8,128)(2,1)} async-done(((bf16[64,4096]{1,0:T(8,128)(2,1)}), bf16[64,256]{1,0:T(8,128)(2,1)}) %reduce-scatter.2.cloned.1.call-update) | async-done | bytes 32784 | tf_op jit(solution)/shard_map/while/body/eval_jaxpr/reduce_scatter | solution.py:114
  828.7 32.0 %all_gather.11 = bf16[64,4096]{1,0:T(8,128)(2,1)S(1)} all-gather(bf16[64,256]{1,0:T(8,128)(2,1)} %reduce-scatter.2.cloned.1.call-done), channel_id=1, replica_groups=mesh['section'=16,'dp'=16] {'dp'}, dimensions={1}, use_global_device_ids=true | all-gather | bytes 557056 | tf_op jit(solution)/shard_map/while/body/eval_jaxpr/all_gather | solution.py:135
  892.6 70.7 %reduce-scatter.2.cloned.1.call-done = bf16[64,256]{1,0:T(8,128)(2,1)} async-done(((bf16[64,4096]{1,0:T(8,128)(2,1)}), bf16[64,256]{1,0:T(8,128)(2,1)}) %reduce-scatter.2.cloned.1.call-update) | async-done | bytes 32784 | tf_op jit(solution)/shard_map/while/body/eval_jaxpr/reduce_scatter | solution.py:114
  963.2 32.0 %all_gather.11 = bf16[64,4096]{1,0:T(8,128)(2,1)S(1)} all-gather(bf16[64,256]{1,0:T(8,128)(2,1)} %reduce-scatter.2.cloned.1.call-done), channel_id=1, replica_groups=mesh['section'=16,'dp'=16] {'dp'}, dimensions={1}, use_global_device_ids=true | all-gather | bytes 557056 | tf_op jit(solution)/shard_map/while/body/eval_jaxpr/all_gather | solution.py:135
  1027.1 71.0 %reduce-scatter.2.cloned.1.call-done = bf16[64,256]{1,0:T(8,128)(2,1)} async-done(((bf16[64,4096]{1,0:T(8,128)(2,1)}), bf16[64,256]{1,0:T(8,128)(2,1)}) %reduce-scatter.2.cloned.1.call-update) | async-done | bytes 32784 | tf_op jit(solution)/shard_map/while/body/eval_jaxpr/reduce_scatter | solution.py:114
  1098.1 32.0 %all_gather.11 = bf16[64,4096]{1,0:T(8,128)(2,1)S(1)} all-gather(bf16[64,256]{1,0:T(8,128)(2,1)} %reduce-scatter.2.cloned.1.call-done), channel_id=1, replica_groups=mesh['section'=16,'dp'=16] {'dp'}, dimensions={1}, use_global_device_ids=true | all-gather | bytes 557056 | tf_op jit(solution)/shard_map/while/body/eval_jaxpr/all_gather | solution.py:135
  1161.9 71.0 %reduce-scatter.2.cloned.1.call-done = bf16[64,256]{1,0:T(8,128)(2,1)} async-done(((bf16[64,4096]{1,0:T(8,128)(2,1)}), bf16[64,256]{1,0:T(8,128)(2,1)}) %reduce-scatter.2.cloned.1.call-update) | async-done | bytes 32784 | tf_op jit(solution)/shard_map/while/body/eval_jaxpr/reduce_scatter | solution.py:114
  1296.8 71.1 %reduce-scatter.2.cloned.1.call-done = bf16[64,256]{1,0:T(8,128)(2,1)} async-done(((bf16[64,4096]{1,0:T(8,128)(2,1)}), bf16[64,256]{1,0:T(8,128)(2,1)}) %reduce-scatter.2.cloned.1.call-update) | async-done | bytes 32784 | tf_op jit(solution)/shard_map/while/body/eval_jaxpr/reduce_scatter | solution.py:114
  1367.9 32.0 %all_gather.11 = bf16[64,4096]{1,0:T(8,128)(2,1)S(1)} all-gather(bf16[64,256]{1,0:T(8,128)(2,1)} %reduce-scatter.2.cloned.1.call-done), channel_id=1, replica_groups=mesh['section'=16,'dp'=16] {'dp'}, dimensions={1}, use_global_device_ids=true | all-gather | bytes 557056 | tf_op jit(solution)/shard_map/while/body/eval_jaxpr/all_gather | solution.py:135
  1431.7 71.0 %reduce-scatter.2.cloned.1.call-done = bf16[64,256]{1,0:T(8,128)(2,1)} async-done(((bf16[64,4096]{1,0:T(8,128)(2,1)}), bf16[64,256]{1,0:T(8,128)(2,1)}) %reduce-scatter.2.cloned.1.call-update) | async-done | bytes 32784 | tf_op jit(solution)/shard_map/while/body/eval_jaxpr/reduce_scatter | solution.py:114
  1502.7 32.0 %all_gather.11 = bf16[64,4096]{1,0:T(8,128)(2,1)S(1)} all-gather(bf16[64,256]{1,0:T(8,128)(2,1)} %reduce-scatter.2.cloned.1.call-done), channel_id=1, replica_groups=mesh['section'=16,'dp'=16] {'dp'}, dimensions={1}, use_global_device_ids=true | all-gather | bytes 557056 | tf_op jit(solution)/shard_map/while/body/eval_jaxpr/all_gather | solution.py:135
  1566.6 70.7 %reduce-scatter.2.cloned.1.call-done = bf16[64,256]{1,0:T(8,128)(2,1)} async-done(((bf16[64,4096]{1,0:T(8,128)(2,1)}), bf16[64,256]{1,0:T(8,128)(2,1)}) %reduce-scatter.2.cloned.1.call-update) | async-done | bytes 32784 | tf_op jit(solution)/shard_map/while/body/eval_jaxpr/reduce_scatter | solution.py:114
  1637.2 32.0 %all_gather.11 = bf16[64,4096]{1,0:T(8,128)(2,1)S(1)} all-gather(bf16[64,256]{1,0:T(8,128)(2,1)} %reduce-scatter.2.cloned.1.call-done), channel_id=1, replica_groups=mesh['section'=16,'dp'=16] {'dp'}, dimensions={1}, use_global_device_ids=true | all-gather | bytes 557056 | tf_op jit(solution)/shard_map/while/body/eval_jaxpr/all_gather | solution.py:135
  1701.1 71.1 %reduce-scatter.2.cloned.1.call-done = bf16[64,256]{1,0:T(8,128)(2,1)} async-done(((bf16[64,4096]{1,0:T(8,128)(2,1)}), bf16[64,256]{1,0:T(8,128)(2,1)}) %reduce-scatter.2.cloned.1.call-update) | async-done | bytes 32784 | tf_op jit(solution)/shard_map/while/body/eval_jaxpr/reduce_scatter | solution.py:114
  1836.0 71.0 %reduce-scatter.2.cloned.1.call-done = bf16[64,256]{1,0:T(8,128)(2,1)} async-done(((bf16[64,4096]{1,0:T(8,128)(2,1)}), bf16[64,256]{1,0:T(8,128)(2,1)}) %reduce-scatter.2.cloned.1.call-update) | async-done | bytes 32784 | tf_op jit(solution)/shard_map/while/body/eval_jaxpr/reduce_scatter | solution.py:114
  1907.0 32.0 %all_gather.11 = bf16[64,4096]{1,0:T(8,128)(2,1)S(1)} all-gather(bf16[64,256]{1,0:T(8,128)(2,1)} %reduce-scatter.2.cloned.1.call-done), channel_id=1, replica_groups=mesh['section'=16,'dp'=16] {'dp'}, dimensions={1}, use_global_device_ids=true | all-gather | bytes 557056 | tf_op jit(solution)/shard_map/while/body/eval_jaxpr/all_gather | solution.py:135
  1970.9 71.0 %reduce-scatter.2.cloned.1.call-done = bf16[64,256]{1,0:T(8,128)(2,1)} async-done(((bf16[64,4096]{1,0:T(8,128)(2,1)}), bf16[64,256]{1,0:T(8,128)(2,1)}) %reduce-scatter.2.cloned.1.call-update) | async-done | bytes 32784 | tf_op jit(solution)/shard_map/while/body/eval_jaxpr/reduce_scatter | solution.py:114
  2041.9 32.0 %all_gather.11 = bf16[64,4096]{1,0:T(8,128)(2,1)S(1)} all-gather(bf16[64,256]{1,0:T(8,128)(2,1)} %reduce-scatter.2.cloned.1.call-done), channel_id=1, replica_groups=mesh['section'=16,'dp'=16] {'dp'}, dimensions={1}, use_global_device_ids=true | all-gather | bytes 557056 | tf_op jit(solution)/shard_map/while/body/eval_jaxpr/all_gather | solution.py:135
  2105.7 71.0 %reduce-scatter.2.cloned.1.call-done = bf16[64,256]{1,0:T(8,128)(2,1)} async-done(((bf16[64,4096]{1,0:T(8,128)(2,1)}), bf16[64,256]{1,0:T(8,128)(2,1)}) %reduce-scatter.2.cloned.1.call-update) | async-done | bytes 32784 | tf_op jit(solution)/shard_map/while/body/eval_jaxpr/reduce_scatter | solution.py:114
  2176.7 32.0 %all_gather.11 = bf16[64,4096]{1,0:T(8,128)(2,1)S(1)} all-gather(bf16[64,256]{1,0:T(8,128)(2,1)} %reduce-scatter.2.cloned.1.call-done), channel_id=1, replica_groups=mesh['section'=16,'dp'=16] {'dp'}, dimensions={1}, use_global_device_ids=true | all-gather | bytes 557056 | tf_op jit(solution)/shard_map/while/body/eval_jaxpr/all_gather | solution.py:135
  2240.6 71.0 %reduce-scatter.2.cloned.1.call-done = bf16[64,256]{1,0:T(8,128)(2,1)} async-done(((bf16[64,4096]{1,0:T(8,128)(2,1)}), bf16[64,256]{1,0:T(8,128)(2,1)}) %reduce-scatter.2.cloned.1.call-update) | async-done | bytes 32784 | tf_op jit(solution)/shard_map/while/body/eval_jaxpr/reduce_scatter | solution.py:114
  2311.6 32.0 %all_gather.11 = bf16[64,4096]{1,0:T(8,128)(2,1)S(1)} all-gather(bf16[64,256]{1,0:T(8,128)(2,1)} %reduce-scatter.2.cloned.1.call-done), channel_id=1, replica_groups=mesh['section'=16,'dp'=16] {'dp'}, dimensions={1}, use_global_device_ids=true | all-gather | bytes 557056 | tf_op jit(solution)/shard_map/while/body/eval_jaxpr/all_gather | solution.py:135
  (562 shorter events, 681.6 us)
Async XLA Ops:
  10.8 51.9 %collective-permute-start.2 = (bf16[4096,128]{0,1:T(8,128)(2,1)S(1)}, bf16[4096,128]{0,1:T(8,128)(2,1)S(1)}, u32[]{:S(2)}, u32[]{:S(2)}) collective-permute-start(bf16[4096,128]{0,1:T(8,128)(2,1)S(1)} %maximum_select_fusion.1), channel_id=1, source_target_pairs={{0,2},{1,3},{2,0},{3,1},{4,6},{5,7},{6,4},{7,5},{8,10},{9,11},{10,... | collective-permute-start | bytes 3145736 | tf_op jit(solution)/shard_map/ppermute | solution.py:14
  67.9 87.2 %reduce-scatter.2.cloned.1.call-start = ((), (), s32[]{:S(2)}) async-start(), calls=%async_computation.1 | async-start | bytes 557056 | tf_op jit(solution)/shard_map/while/body/eval_jaxpr/reduce_scatter | solution.py:114
  189.8 18.2 collective-permute-start
  208.0 82.0 %reduce-scatter.2.cloned.1.call-start = ((), (), s32[]{:S(2)}) async-start(), calls=%async_computation.1 | async-start | bytes 557056 | tf_op jit(solution)/shard_map/while/body/eval_jaxpr/reduce_scatter | solution.py:114
  324.7 18.2 collective-permute-start
  342.9 81.9 %reduce-scatter.2.cloned.1.call-start = ((), (), s32[]{:S(2)}) async-start(), calls=%async_computation.1 | async-start | bytes 557056 | tf_op jit(solution)/shard_map/while/body/eval_jaxpr/reduce_scatter | solution.py:114
  459.5 18.2 collective-permute-start
  477.7 81.6 %reduce-scatter.2.cloned.1.call-start = ((), (), s32[]{:S(2)}) async-start(), calls=%async_computation.1 | async-start | bytes 557056 | tf_op jit(solution)/shard_map/while/body/eval_jaxpr/reduce_scatter | solution.py:114
  594.1 18.2 collective-permute-start
  612.3 81.9 %reduce-scatter.2.cloned.1.call-start = ((), (), s32[]{:S(2)}) async-start(), calls=%async_computation.1 | async-start | bytes 557056 | tf_op jit(solution)/shard_map/while/body/eval_jaxpr/reduce_scatter | solution.py:114
  729.0 18.2 collective-permute-start
  747.1 81.5 %reduce-scatter.2.cloned.1.call-start = ((), (), s32[]{:S(2)}) async-start(), calls=%async_computation.1 | async-start | bytes 557056 | tf_op jit(solution)/shard_map/while/body/eval_jaxpr/reduce_scatter | solution.py:114
  863.5 18.2 collective-permute-start
  881.6 81.6 %reduce-scatter.2.cloned.1.call-start = ((), (), s32[]{:S(2)}) async-start(), calls=%async_computation.1 | async-start | bytes 557056 | tf_op jit(solution)/shard_map/while/body/eval_jaxpr/reduce_scatter | solution.py:114
  998.0 18.2 collective-permute-start
  1016.2 81.9 %reduce-scatter.2.cloned.1.call-start = ((), (), s32[]{:S(2)}) async-start(), calls=%async_computation.1 | async-start | bytes 557056 | tf_op jit(solution)/shard_map/while/body/eval_jaxpr/reduce_scatter | solution.py:114
  1132.8 18.2 collective-permute-start
  1151.0 81.9 %reduce-scatter.2.cloned.1.call-start = ((), (), s32[]{:S(2)}) async-start(), calls=%async_computation.1 | async-start | bytes 557056 | tf_op jit(solution)/shard_map/while/body/eval_jaxpr/reduce_scatter | solution.py:114
  1267.7 18.2 collective-permute-start
  1285.9 82.0 %reduce-scatter.2.cloned.1.call-start = ((), (), s32[]{:S(2)}) async-start(), calls=%async_computation.1 | async-start | bytes 557056 | tf_op jit(solution)/shard_map/while/body/eval_jaxpr/reduce_scatter | solution.py:114
  1402.6 18.2 collective-permute-start
  1420.8 81.9 %reduce-scatter.2.cloned.1.call-start = ((), (), s32[]{:S(2)}) async-start(), calls=%async_computation.1 | async-start | bytes 557056 | tf_op jit(solution)/shard_map/while/body/eval_jaxpr/reduce_scatter | solution.py:114
  1537.5 18.2 collective-permute-start
  1555.6 81.6 %reduce-scatter.2.cloned.1.call-start = ((), (), s32[]{:S(2)}) async-start(), calls=%async_computation.1 | async-start | bytes 557056 | tf_op jit(solution)/shard_map/while/body/eval_jaxpr/reduce_scatter | solution.py:114
  1672.0 18.2 collective-permute-start
  1690.2 82.0 %reduce-scatter.2.cloned.1.call-start = ((), (), s32[]{:S(2)}) async-start(), calls=%async_computation.1 | async-start | bytes 557056 | tf_op jit(solution)/shard_map/while/body/eval_jaxpr/reduce_scatter | solution.py:114
  1806.9 18.2 collective-permute-start
  1825.1 81.9 %reduce-scatter.2.cloned.1.call-start = ((), (), s32[]{:S(2)}) async-start(), calls=%async_computation.1 | async-start | bytes 557056 | tf_op jit(solution)/shard_map/while/body/eval_jaxpr/reduce_scatter | solution.py:114
  1941.8 18.2 collective-permute-start
  1960.0 81.9 %reduce-scatter.2.cloned.1.call-start = ((), (), s32[]{:S(2)}) async-start(), calls=%async_computation.1 | async-start | bytes 557056 | tf_op jit(solution)/shard_map/while/body/eval_jaxpr/reduce_scatter | solution.py:114
  2094.8 81.9 %reduce-scatter.2.cloned.1.call-start = ((), (), s32[]{:S(2)}) async-start(), calls=%async_computation.1 | async-start | bytes 557056 | tf_op jit(solution)/shard_map/while/body/eval_jaxpr/reduce_scatter | solution.py:114
  2229.7 81.9 %reduce-scatter.2.cloned.1.call-start = ((), (), s32[]{:S(2)}) async-start(), calls=%async_computation.1 | async-start | bytes 557056 | tf_op jit(solution)/shard_map/while/body/eval_jaxpr/reduce_scatter | solution.py:114
  (57 other events, 209.0 us)
Sparse Core Ops, SparseCore 0:
  78.8 76.2 reduce-scatter.1
  218.8 71.1 reduce-scatter.1
  353.7 71.0 reduce-scatter.1
  488.5 70.7 reduce-scatter.1
  623.1 71.0 reduce-scatter.1
  757.9 70.6 reduce-scatter.1
  892.5 70.7 reduce-scatter.1
  1027.0 71.0 reduce-scatter.1
  1161.8 71.0 reduce-scatter.1
  1296.7 71.1 reduce-scatter.1
  1431.6 71.0 reduce-scatter.1
  1566.4 70.7 reduce-scatter.1
  1701.0 71.1 reduce-scatter.1
  1835.9 71.0 reduce-scatter.1
  1970.8 71.0 reduce-scatter.1
  2105.6 71.0 reduce-scatter.1
  2240.5 71.0 reduce-scatter.1
where the time goes:
time: 2380 us; the launch traced here: 2370 us
  waiting for transfers between devices  1440 us (61%)
  blocking collectives  544 us (23%)
  matrix products  239 us (10%)
  other arithmetic  75.6 us (3%)
  starting transfers between devices  52.2 us (2%)
    reduce_scatter x17, waiting for transfers between devices, backward_step(): lax.psum_scatter(partial_value.astype(jnp.bfloat16), 'dp', scatter_dimens...  1210 us
    all_gather x17, blocking collectives, tick_whole(): lax.all_gather(norm_part, 'dp', axis=1, tiled=True).astype(jnp.float32)  544 us
    ppermute x17, waiting for transfers between devices, shifted(): return lax.ppermute(value, axis, pairs)  180 us
    dot_general x17, matrix products, layer_terms(): jnp.einsum('tk,tc->kc', attended_flat, upstream, preferred_element_type=j...  81.8 us
    ppermute x2, waiting for transfers between devices, swapped(): return lax.ppermute(value, axis, pairs)  47.8 us
  transfers between devices with their start and end apart: 36, of which 36 were waited for; matrix products, arithmetic and copies ran while one was open for 4% of the time, Pallas kernels for 0%

commit v1 on v0

--- a/solution.py
+++ b/solution.py
@@ -132,7 +132,9 @@
         norm_part, upstream, weight_grad, inputs_f, inverse_rms, micro_clip, active = backward_step(
             step_pos, incoming
         )
-        norm_grad = lax.all_gather(norm_part, "dp", axis=1, tiled=True).astype(jnp.float32)
+        norm_grad = jnp.concatenate(
+            lax.all_to_all(jnp.stack([norm_part] * lax.axis_size("dp")), "dp", 0, 0), axis=1
+        ).astype(jnp.float32)
         scaled = norm_grad * gain
         row_stat = jnp.sum(scaled * inputs_f, axis=-1, keepdims=True) / width
         result = (

time: 2380 us -> 2300 us (0.966)
  blocking collectives: 544 us -> 0 us
  waiting for transfers between devices: 1440 us -> 1790 us
  starting transfers between devices: 52.2 us -> 141 us
  local copies, waits for them, and re-layouts: 4.46 us -> 69.1 us
  matrix products: 239 us -> 179 us
    all_gather x17 -> x0, blocking collectives: 544 us -> none  [tick_whole(): lax.all_gather(norm_part, 'dp', axis=1, tiled=True).astype(jnp.float32)]
    all_to_all x0 -> x17, waiting for transfers between devices: none -> 302 us  [tick_whole(): lax.all_to_all(jnp.stack([norm_part] * lax.axis_size('dp')), 'dp', 0, 0)]
    all_to_all x0 -> x17, starting transfers between devices: none -> 88.5 us  [tick_whole(): lax.all_to_all(jnp.stack([norm_part] * lax.axis_size('dp')), 'dp', 0, 0)]
    dot_general x17, matrix products: 81.8 us -> 21.7 us  [layer_terms(): jnp.einsum('tk,tc->kc', attended_flat, upstream, preferred_element_type=j...]
    ppermute x17, waiting for transfers between devices: 180 us -> 223 us  [shifted(): return lax.ppermute(value, axis, pairs)]
    while x102 -> x238, local copies, waits for them, and re-layouts: 0.32 us -> 37.8 us
    another operation x0 -> x17, local copies, waits for them, and re-layouts: none -> 27.3 us  [tick_whole(): jnp.stack([norm_part] * lax.axis_size('dp'))]
    convert_element_type x0 -> x34, other arithmetic: none -> 24.2 us  [the longest x17 19 us: layer_terms(): inputs_f = inputs.astype(jnp.float32)]
  transfers between devices with their start and end apart: 36 -> 53, of which waited for: 36 -> 53; matrix products, arithmetic and copies ran while one was open for 4% -> 3% of each run, Pallas kernels for 0% -> 0%
where the time goes in v1:
time: 2300 us; the launch traced here: 2290 us
  waiting for transfers between devices  1790 us (78%)
  matrix products  179 us (8%)
  starting transfers between devices  141 us (6%)
  other arithmetic  92.4 us (4%)
  local copies, waits for them, and re-layouts  69.1 us (3%)
    reduce_scatter x17, waiting for transfers between devices, backward_step(): lax.psum_scatter(partial_value.astype(jnp.bfloat16), 'dp', scatter_dimens...  1220 us
    all_to_all x17, waiting for transfers between devices, tick_whole(): lax.all_to_all(jnp.stack([norm_part] * lax.axis_size('dp')), 'dp', 0, 0)  302 us
    ppermute x17, waiting for transfers between devices, shifted(): return lax.ppermute(value, axis, pairs)  223 us
    all_to_all x17, starting transfers between devices, tick_whole(): lax.all_to_all(jnp.stack([norm_part] * lax.axis_size('dp')), 'dp', 0, 0)  88.5 us
    ppermute x2, waiting for transfers between devices, swapped(): return lax.ppermute(value, axis, pairs)  47.8 us
    ppermute x17, starting transfers between devices, shifted(): return lax.ppermute(value, axis, pairs)  46.6 us
  transfers between devices with their start and end apart: 53, of which 53 were waited for; matrix products, arithmetic and copies ran while one was open for 3% of the time, Pallas kernels for 0%

profile of v1, /device:TPU:88, one launch (start us, length us, event | category | flops | bytes accessed | tf_op | source)
XLA Modules:
  0.0 2287.8 jit_solution(13279013993601131041)
XLA Ops:
  17.0 45.7 %collective-permute-done.2 = bf16[4096,128]{0,1:T(8,128)(2,1)S(1)} collective-permute-done((bf16[4096,128]{0,1:T(8,128)(2,1)S(1)}, bf16[4096,128]{0,1:T(8,128)(2,1)S(1)}, u32[]{:S(2)}, u32[]{:S(2)}) %collective-permute-start.2) | collective-permute-done | bytes 1048608 | tf_op jit(solution)/shard_map/ppermute | solution.py:14
  67.9 2212.7 %while.21 = (s32[]{:T(128)}, bf16[64,4096]{1,0:T(8,128)(2,1)S(1)}, bf16[2,64,256]{2,1,0:T(8,128)(2,1)S(1)}, f32[256,4096]{1,0:T(8,128)}, pred[]{:T(512)}, /*inde...) while((s32[]{:T(128)}, bf16[64,4096]{1,0:T(8,128)(2,1)S(1)}, ...), condition=%wide.wide.region_7.8_spmd.clone, body=%wide.wide.region_0.7_spmd.clone.sunk | while | flops 828969088 | bytes 102944800 | solution.py:153
  78.6 76.4 %reduce-scatter.2.cloned.1.call-done = bf16[64,256]{1,0:T(8,128)(2,1)} async-done(((bf16[64,4096]{1,0:T(8,128)(2,1)}), bf16[64,256]{1,0:T(8,128)(2,1)}) %reduce-scatter.2.cloned.1.call-update) | async-done | bytes 32784 | tf_op jit(solution)/shard_map/while/body/eval_jaxpr/reduce_scatter | solution.py:114
  164.6 17.8 all-to-all-done
  213.7 71.2 %reduce-scatter.2.cloned.1.call-done = bf16[64,256]{1,0:T(8,128)(2,1)} async-done(((bf16[64,4096]{1,0:T(8,128)(2,1)}), bf16[64,256]{1,0:T(8,128)(2,1)}) %reduce-scatter.2.cloned.1.call-update) | async-done | bytes 32784 | tf_op jit(solution)/shard_map/while/body/eval_jaxpr/reduce_scatter | solution.py:114
  294.4 17.8 all-to-all-done
  343.5 71.2 %reduce-scatter.2.cloned.1.call-done = bf16[64,256]{1,0:T(8,128)(2,1)} async-done(((bf16[64,4096]{1,0:T(8,128)(2,1)}), bf16[64,256]{1,0:T(8,128)(2,1)}) %reduce-scatter.2.cloned.1.call-update) | async-done | bytes 32784 | tf_op jit(solution)/shard_map/while/body/eval_jaxpr/reduce_scatter | solution.py:114
  424.2 17.8 all-to-all-done
  473.4 71.2 %reduce-scatter.2.cloned.1.call-done = bf16[64,256]{1,0:T(8,128)(2,1)} async-done(((bf16[64,4096]{1,0:T(8,128)(2,1)}), bf16[64,256]{1,0:T(8,128)(2,1)}) %reduce-scatter.2.cloned.1.call-update) | async-done | bytes 32784 | tf_op jit(solution)/shard_map/while/body/eval_jaxpr/reduce_scatter | solution.py:114
  554.0 17.8 all-to-all-done
  603.2 71.2 %reduce-scatter.2.cloned.1.call-done = bf16[64,256]{1,0:T(8,128)(2,1)} async-done(((bf16[64,4096]{1,0:T(8,128)(2,1)}), bf16[64,256]{1,0:T(8,128)(2,1)}) %reduce-scatter.2.cloned.1.call-update) | async-done | bytes 32784 | tf_op jit(solution)/shard_map/while/body/eval_jaxpr/reduce_scatter | solution.py:114
  683.8 17.8 all-to-all-done
  733.0 71.2 %reduce-scatter.2.cloned.1.call-done = bf16[64,256]{1,0:T(8,128)(2,1)} async-done(((bf16[64,4096]{1,0:T(8,128)(2,1)}), bf16[64,256]{1,0:T(8,128)(2,1)}) %reduce-scatter.2.cloned.1.call-update) | async-done | bytes 32784 | tf_op jit(solution)/shard_map/while/body/eval_jaxpr/reduce_scatter | solution.py:114
  813.7 17.8 all-to-all-done
  862.8 71.2 %reduce-scatter.2.cloned.1.call-done = bf16[64,256]{1,0:T(8,128)(2,1)} async-done(((bf16[64,4096]{1,0:T(8,128)(2,1)}), bf16[64,256]{1,0:T(8,128)(2,1)}) %reduce-scatter.2.cloned.1.call-update) | async-done | bytes 32784 | tf_op jit(solution)/shard_map/while/body/eval_jaxpr/reduce_scatter | solution.py:114
  943.5 17.8 all-to-all-done
  992.7 71.2 %reduce-scatter.2.cloned.1.call-done = bf16[64,256]{1,0:T(8,128)(2,1)} async-done(((bf16[64,4096]{1,0:T(8,128)(2,1)}), bf16[64,256]{1,0:T(8,128)(2,1)}) %reduce-scatter.2.cloned.1.call-update) | async-done | bytes 32784 | tf_op jit(solution)/shard_map/while/body/eval_jaxpr/reduce_scatter | solution.py:114
  1073.4 17.8 all-to-all-done
  1122.5 71.2 %reduce-scatter.2.cloned.1.call-done = bf16[64,256]{1,0:T(8,128)(2,1)} async-done(((bf16[64,4096]{1,0:T(8,128)(2,1)}), bf16[64,256]{1,0:T(8,128)(2,1)}) %reduce-scatter.2.cloned.1.call-update) | async-done | bytes 32784 | tf_op jit(solution)/shard_map/while/body/eval_jaxpr/reduce_scatter | solution.py:114
  1203.2 17.8 all-to-all-done
  1252.4 71.2 %reduce-scatter.2.cloned.1.call-done = bf16[64,256]{1,0:T(8,128)(2,1)} async-done(((bf16[64,4096]{1,0:T(8,128)(2,1)}), bf16[64,256]{1,0:T(8,128)(2,1)}) %reduce-scatter.2.cloned.1.call-update) | async-done | bytes 32784 | tf_op jit(solution)/shard_map/while/body/eval_jaxpr/reduce_scatter | solution.py:114
  1333.1 17.8 all-to-all-done
  1382.3 71.2 %reduce-scatter.2.cloned.1.call-done = bf16[64,256]{1,0:T(8,128)(2,1)} async-done(((bf16[64,4096]{1,0:T(8,128)(2,1)}), bf16[64,256]{1,0:T(8,128)(2,1)}) %reduce-scatter.2.cloned.1.call-update) | async-done | bytes 32784 | tf_op jit(solution)/shard_map/while/body/eval_jaxpr/reduce_scatter | solution.py:114
  1463.0 17.8 all-to-all-done
  1512.1 71.2 %reduce-scatter.2.cloned.1.call-done = bf16[64,256]{1,0:T(8,128)(2,1)} async-done(((bf16[64,4096]{1,0:T(8,128)(2,1)}), bf16[64,256]{1,0:T(8,128)(2,1)}) %reduce-scatter.2.cloned.1.call-update) | async-done | bytes 32784 | tf_op jit(solution)/shard_map/while/body/eval_jaxpr/reduce_scatter | solution.py:114
  1592.8 17.8 all-to-all-done
  1642.0 71.2 %reduce-scatter.2.cloned.1.call-done = bf16[64,256]{1,0:T(8,128)(2,1)} async-done(((bf16[64,4096]{1,0:T(8,128)(2,1)}), bf16[64,256]{1,0:T(8,128)(2,1)}) %reduce-scatter.2.cloned.1.call-update) | async-done | bytes 32784 | tf_op jit(solution)/shard_map/while/body/eval_jaxpr/reduce_scatter | solution.py:114
  1722.7 17.8 all-to-all-done
  1771.8 71.2 %reduce-scatter.2.cloned.1.call-done = bf16[64,256]{1,0:T(8,128)(2,1)} async-done(((bf16[64,4096]{1,0:T(8,128)(2,1)}), bf16[64,256]{1,0:T(8,128)(2,1)}) %reduce-scatter.2.cloned.1.call-update) | async-done | bytes 32784 | tf_op jit(solution)/shard_map/while/body/eval_jaxpr/reduce_scatter | solution.py:114
  1901.7 71.3 %reduce-scatter.2.cloned.1.call-done = bf16[64,256]{1,0:T(8,128)(2,1)} async-done(((bf16[64,4096]{1,0:T(8,128)(2,1)}), bf16[64,256]{1,0:T(8,128)(2,1)}) %reduce-scatter.2.cloned.1.call-update) | async-done | bytes 32784 | tf_op jit(solution)/shard_map/while/body/eval_jaxpr/reduce_scatter | solution.py:114
  2031.6 71.3 %reduce-scatter.2.cloned.1.call-done = bf16[64,256]{1,0:T(8,128)(2,1)} async-done(((bf16[64,4096]{1,0:T(8,128)(2,1)}), bf16[64,256]{1,0:T(8,128)(2,1)}) %reduce-scatter.2.cloned.1.call-update) | async-done | bytes 32784 | tf_op jit(solution)/shard_map/while/body/eval_jaxpr/reduce_scatter | solution.py:114
  2161.5 71.2 %reduce-scatter.2.cloned.1.call-done = bf16[64,256]{1,0:T(8,128)(2,1)} async-done(((bf16[64,4096]{1,0:T(8,128)(2,1)}), bf16[64,256]{1,0:T(8,128)(2,1)}) %reduce-scatter.2.cloned.1.call-update) | async-done | bytes 32784 | tf_op jit(solution)/shard_map/while/body/eval_jaxpr/reduce_scatter | solution.py:114
  (767 shorter events, 777.0 us)
Async XLA Ops:
  10.8 51.9 %collective-permute-start.2 = (bf16[4096,128]{0,1:T(8,128)(2,1)S(1)}, bf16[4096,128]{0,1:T(8,128)(2,1)S(1)}, u32[]{:S(2)}, u32[]{:S(2)}) collective-permute-start(bf16[4096,128]{0,1:T(8,128)(2,1)S(1)} %maximum_select_fusion.1), channel_id=1, source_target_pairs={{0,2},{1,3},{2,0},{3,1},{4,6},{5,7},{6,4},{7,5},{8,10},{9,11},{10,... | collective-permute-start | bytes 3145736 | tf_op jit(solution)/shard_map/ppermute | solution.py:14
  67.9 87.2 %reduce-scatter.2.cloned.1.call-start = ((), (), s32[]{:S(2)}) async-start(), calls=%async_computation.2 | async-start | bytes 557056 | tf_op jit(solution)/shard_map/while/body/eval_jaxpr/reduce_scatter | solution.py:114
  156.7 25.6 %all-to-all-start = ((bf16[16,64,256]{2,1,0:T(8,128)(2,1)}), bf16[16,64,256]{2,1,0:T(8,128)(2,1)S(1)}, u32[]{:S(2)}, u32[]{:S(2)}) async-start(bf16[16,64,256]{2,1,0:T(8,128)(2,1)} %stack.9), calls=%async_computation.1 | async-start | bytes 1048576 | tf_op jit(solution)/shard_map/while/body/eval_jaxpr/all_to_all | solution.py:136
  203.0 81.9 %reduce-scatter.2.cloned.1.call-start = ((), (), s32[]{:S(2)}) async-start(), calls=%async_computation.2 | async-start | bytes 557056 | tf_op jit(solution)/shard_map/while/body/eval_jaxpr/reduce_scatter | solution.py:114
  286.5 25.6 %all-to-all-start = ((bf16[16,64,256]{2,1,0:T(8,128)(2,1)}), bf16[16,64,256]{2,1,0:T(8,128)(2,1)S(1)}, u32[]{:S(2)}, u32[]{:S(2)}) async-start(bf16[16,64,256]{2,1,0:T(8,128)(2,1)} %stack.9), calls=%async_computation.1 | async-start | bytes 1048576 | tf_op jit(solution)/shard_map/while/body/eval_jaxpr/all_to_all | solution.py:136
  332.8 81.9 %reduce-scatter.2.cloned.1.call-start = ((), (), s32[]{:S(2)}) async-start(), calls=%async_computation.2 | async-start | bytes 557056 | tf_op jit(solution)/shard_map/while/body/eval_jaxpr/reduce_scatter | solution.py:114
  462.7 81.9 %reduce-scatter.2.cloned.1.call-start = ((), (), s32[]{:S(2)}) async-start(), calls=%async_computation.2 | async-start | bytes 557056 | tf_op jit(solution)/shard_map/while/body/eval_jaxpr/reduce_scatter | solution.py:114
  546.2 25.6 %all-to-all-start = ((bf16[16,64,256]{2,1,0:T(8,128)(2,1)}), bf16[16,64,256]{2,1,0:T(8,128)(2,1)S(1)}, u32[]{:S(2)}, u32[]{:S(2)}) async-start(bf16[16,64,256]{2,1,0:T(8,128)(2,1)} %stack.9), calls=%async_computation.1 | async-start | bytes 1048576 | tf_op jit(solution)/shard_map/while/body/eval_jaxpr/all_to_all | solution.py:136
  592.5 81.9 %reduce-scatter.2.cloned.1.call-start = ((), (), s32[]{:S(2)}) async-start(), calls=%async_computation.2 | async-start | bytes 557056 | tf_op jit(solution)/shard_map/while/body/eval_jaxpr/reduce_scatter | solution.py:114
  722.3 81.9 %reduce-scatter.2.cloned.1.call-start = ((), (), s32[]{:S(2)}) async-start(), calls=%async_computation.2 | async-start | bytes 557056 | tf_op jit(solution)/shard_map/while/body/eval_jaxpr/reduce_scatter | solution.py:114
  805.8 25.6 %all-to-all-start = ((bf16[16,64,256]{2,1,0:T(8,128)(2,1)}), bf16[16,64,256]{2,1,0:T(8,128)(2,1)S(1)}, u32[]{:S(2)}, u32[]{:S(2)}) async-start(bf16[16,64,256]{2,1,0:T(8,128)(2,1)} %stack.9), calls=%async_computation.1 | async-start | bytes 1048576 | tf_op jit(solution)/shard_map/while/body/eval_jaxpr/all_to_all | solution.py:136
  852.2 81.9 %reduce-scatter.2.cloned.1.call-start = ((), (), s32[]{:S(2)}) async-start(), calls=%async_computation.2 | async-start | bytes 557056 | tf_op jit(solution)/shard_map/while/body/eval_jaxpr/reduce_scatter | solution.py:114
  935.7 25.6 %all-to-all-start = ((bf16[16,64,256]{2,1,0:T(8,128)(2,1)}), bf16[16,64,256]{2,1,0:T(8,128)(2,1)S(1)}, u32[]{:S(2)}, u32[]{:S(2)}) async-start(bf16[16,64,256]{2,1,0:T(8,128)(2,1)} %stack.9), calls=%async_computation.1 | async-start | bytes 1048576 | tf_op jit(solution)/shard_map/while/body/eval_jaxpr/all_to_all | solution.py:136
  982.0 81.9 %reduce-scatter.2.cloned.1.call-start = ((), (), s32[]{:S(2)}) async-start(), calls=%async_computation.2 | async-start | bytes 557056 | tf_op jit(solution)/shard_map/while/body/eval_jaxpr/reduce_scatter | solution.py:114
  1065.5 25.6 %all-to-all-start = ((bf16[16,64,256]{2,1,0:T(8,128)(2,1)}), bf16[16,64,256]{2,1,0:T(8,128)(2,1)S(1)}, u32[]{:S(2)}, u32[]{:S(2)}) async-start(bf16[16,64,256]{2,1,0:T(8,128)(2,1)} %stack.9), calls=%async_computation.1 | async-start | bytes 1048576 | tf_op jit(solution)/shard_map/while/body/eval_jaxpr/all_to_all | solution.py:136
  1111.8 81.9 %reduce-scatter.2.cloned.1.call-start = ((), (), s32[]{:S(2)}) async-start(), calls=%async_computation.2 | async-start | bytes 557056 | tf_op jit(solution)/shard_map/while/body/eval_jaxpr/reduce_scatter | solution.py:114
  1195.4 25.6 %all-to-all-start = ((bf16[16,64,256]{2,1,0:T(8,128)(2,1)}), bf16[16,64,256]{2,1,0:T(8,128)(2,1)S(1)}, u32[]{:S(2)}, u32[]{:S(2)}) async-start(bf16[16,64,256]{2,1,0:T(8,128)(2,1)} %stack.9), calls=%async_computation.1 | async-start | bytes 1048576 | tf_op jit(solution)/shard_map/while/body/eval_jaxpr/all_to_all | solution.py:136
  1241.7 81.9 %reduce-scatter.2.cloned.1.call-start = ((), (), s32[]{:S(2)}) async-start(), calls=%async_computation.2 | async-start | bytes 557056 | tf_op jit(solution)/shard_map/while/body/eval_jaxpr/reduce_scatter | solution.py:114
  1371.6 81.9 %reduce-scatter.2.cloned.1.call-start = ((), (), s32[]{:S(2)}) async-start(), calls=%async_computation.2 | async-start | bytes 557056 | tf_op jit(solution)/shard_map/while/body/eval_jaxpr/reduce_scatter | solution.py:114
  1455.1 25.6 %all-to-all-start = ((bf16[16,64,256]{2,1,0:T(8,128)(2,1)}), bf16[16,64,256]{2,1,0:T(8,128)(2,1)S(1)}, u32[]{:S(2)}, u32[]{:S(2)}) async-start(bf16[16,64,256]{2,1,0:T(8,128)(2,1)} %stack.9), calls=%async_computation.1 | async-start | bytes 1048576 | tf_op jit(solution)/shard_map/while/body/eval_jaxpr/all_to_all | solution.py:136
  1501.4 81.9 %reduce-scatter.2.cloned.1.call-start = ((), (), s32[]{:S(2)}) async-start(), calls=%async_computation.2 | async-start | bytes 557056 | tf_op jit(solution)/shard_map/while/body/eval_jaxpr/reduce_scatter | solution.py:114
  1585.0 25.6 %all-to-all-start = ((bf16[16,64,256]{2,1,0:T(8,128)(2,1)}), bf16[16,64,256]{2,1,0:T(8,128)(2,1)S(1)}, u32[]{:S(2)}, u32[]{:S(2)}) async-start(bf16[16,64,256]{2,1,0:T(8,128)(2,1)} %stack.9), calls=%async_computation.1 | async-start | bytes 1048576 | tf_op jit(solution)/shard_map/while/body/eval_jaxpr/all_to_all | solution.py:136
  1631.3 81.9 %reduce-scatter.2.cloned.1.call-start = ((), (), s32[]{:S(2)}) async-start(), calls=%async_computation.2 | async-start | bytes 557056 | tf_op jit(solution)/shard_map/while/body/eval_jaxpr/reduce_scatter | solution.py:114
  1714.8 25.6 %all-to-all-start = ((bf16[16,64,256]{2,1,0:T(8,128)(2,1)}), bf16[16,64,256]{2,1,0:T(8,128)(2,1)S(1)}, u32[]{:S(2)}, u32[]{:S(2)}) async-start(bf16[16,64,256]{2,1,0:T(8,128)(2,1)} %stack.9), calls=%async_computation.1 | async-start | bytes 1048576 | tf_op jit(solution)/shard_map/while/body/eval_jaxpr/all_to_all | solution.py:136
  1761.1 81.9 %reduce-scatter.2.cloned.1.call-start = ((), (), s32[]{:S(2)}) async-start(), calls=%async_computation.2 | async-start | bytes 557056 | tf_op jit(solution)/shard_map/while/body/eval_jaxpr/reduce_scatter | solution.py:114
  1844.7 25.6 %all-to-all-start = ((bf16[16,64,256]{2,1,0:T(8,128)(2,1)}), bf16[16,64,256]{2,1,0:T(8,128)(2,1)S(1)}, u32[]{:S(2)}, u32[]{:S(2)}) async-start(bf16[16,64,256]{2,1,0:T(8,128)(2,1)} %stack.9), calls=%async_computation.1 | async-start | bytes 1048576 | tf_op jit(solution)/shard_map/while/body/eval_jaxpr/all_to_all | solution.py:136
  1891.0 82.0 %reduce-scatter.2.cloned.1.call-start = ((), (), s32[]{:S(2)}) async-start(), calls=%async_computation.2 | async-start | bytes 557056 | tf_op jit(solution)/shard_map/while/body/eval_jaxpr/reduce_scatter | solution.py:114
  1974.6 25.6 %all-to-all-start = ((bf16[16,64,256]{2,1,0:T(8,128)(2,1)}), bf16[16,64,256]{2,1,0:T(8,128)(2,1)S(1)}, u32[]{:S(2)}, u32[]{:S(2)}) async-start(bf16[16,64,256]{2,1,0:T(8,128)(2,1)} %stack.9), calls=%async_computation.1 | async-start | bytes 1048576 | tf_op jit(solution)/shard_map/while/body/eval_jaxpr/all_to_all | solution.py:136
  2020.9 82.0 %reduce-scatter.2.cloned.1.call-start = ((), (), s32[]{:S(2)}) async-start(), calls=%async_computation.2 | async-start | bytes 557056 | tf_op jit(solution)/shard_map/while/body/eval_jaxpr/reduce_scatter | solution.py:114
  2104.5 25.6 %all-to-all-start = ((bf16[16,64,256]{2,1,0:T(8,128)(2,1)}), bf16[16,64,256]{2,1,0:T(8,128)(2,1)S(1)}, u32[]{:S(2)}, u32[]{:S(2)}) async-start(bf16[16,64,256]{2,1,0:T(8,128)(2,1)} %stack.9), calls=%async_computation.1 | async-start | bytes 1048576 | tf_op jit(solution)/shard_map/while/body/eval_jaxpr/all_to_all | solution.py:136
  2150.8 81.9 %reduce-scatter.2.cloned.1.call-start = ((), (), s32[]{:S(2)}) async-start(), calls=%async_computation.2 | async-start | bytes 557056 | tf_op jit(solution)/shard_map/while/body/eval_jaxpr/reduce_scatter | solution.py:114
  2234.3 25.6 %all-to-all-start = ((bf16[16,64,256]{2,1,0:T(8,128)(2,1)}), bf16[16,64,256]{2,1,0:T(8,128)(2,1)S(1)}, u32[]{:S(2)}, u32[]{:S(2)}) async-start(bf16[16,64,256]{2,1,0:T(8,128)(2,1)} %stack.9), calls=%async_computation.1 | async-start | bytes 1048576 | tf_op jit(solution)/shard_map/while/body/eval_jaxpr/all_to_all | solution.py:136
  (125 other events, 853.2 us)
Sparse Core Ops, SparseCore 0:
  78.8 76.2 reduce-scatter.1
  213.8 71.0 reduce-scatter.1
  343.7 71.0 reduce-scatter.1
  473.5 71.0 reduce-scatter.1
  603.3 71.0 reduce-scatter.1
  733.1 71.0 reduce-scatter.1
  863.0 71.0 reduce-scatter.1
  992.8 71.0 reduce-scatter.1
  1122.7 71.0 reduce-scatter.1
  1252.5 71.0 reduce-scatter.1
  1382.4 71.0 reduce-scatter.1
  1512.2 71.0 reduce-scatter.1
  1642.1 71.0 reduce-scatter.1
  1772.0 71.0 reduce-scatter.1
  1901.8 71.1 reduce-scatter.1
  2031.7 71.1 reduce-scatter.1
  2161.6 71.0 reduce-scatter.1
